TPU v7x, 512 devices: a whole 4x8x8 slice. The times are simulated.
512 devices in a mesh: mem: 32 (over z, x), geo: 16 (over y, core).
Axes of the slice: x: 4, y: 8, z: 8, core: 2. Of those that a mesh axis runs over, the one named last changes fastest.
Arguments:
- control: float32 [32, 32, 48, 384], P('mem', 'geo'), may hold values from -6 to 6
- kappa_table: float32 [16], replicated, may hold values from 0.02 to 0.24
- kappa_index: int32 [48, 384], replicated, may hold values from 0 to 15
- tile_bounds: int32 [17], replicated, may hold values from 0 to 18432, as said below
- filter_bands: float32 [16, 5, 32], replicated, may hold values from -0.3 to 0.3
- perturbation: bfloat16 [2, 32, 32, 18432], P(None, 'mem', None, 'geo'), may hold values from -6 to 6
Outputs:
- increment: float32 [2, 32, 18432], P(None, 'mem', 'geo')
Inputs may be any that keep to these rules, and one draw needn't show every extreme that they name: tile_bounds[0] is 0, tile_bounds[16] is 18432, and the bounds never fall; tile t holds columns tile_bounds[t] to tile_bounds[t + 1] - 1.
All inputs are finite; a program needn't handle non-finite values.
Results may differ from a plain program's by a relative error of at most 0.005.
Values may be sent and summed in bfloat16 or wider, within the bound.
No kernel may reach another device: no remote copies, remote signals or barrier semaphores. Data moves between devices by JAX's collectives and lax.ppermute only.
A program may use at most 64 MiB of HBM per device.

v0:
```python
import jax
import jax.numpy as jnp
from jax import lax
from jax.sharding import PartitionSpec as P

ITERS = 10


def neighbours(state):
    east = jnp.concatenate([state[..., 1:, :], state[..., -1:, :]], axis=-2)
    west = jnp.concatenate([state[..., :1, :], state[..., :-1, :]], axis=-2)
    north = jnp.concatenate([state[..., 1:], state[..., -1:]], axis=-1)
    south = jnp.concatenate([state[..., :1], state[..., :-1]], axis=-1)
    return (east, west, north, south)


def face_weights(kappa_field):
    return tuple((0.5 * (kappa_field + other) for other in neighbours(kappa_field)))


def diffuse_step(state, weights):
    east, west, north, south = neighbours(state)
    update = weights[0] * (east - state) + weights[1] * (west - state)
    update = update + weights[2] * (north - state) + weights[3] * (south - state)
    return state + update


def vertical_filter(values, coefficients):
    levels = values.shape[0]
    padded = jnp.pad(values, ((2, 2), (0, 0)))
    result = values
    for offset in range(5):
        result = result + coefficients[offset] * padded[offset : offset + levels]
    return result


def body(control, kappa_table, kappa_index, tile_bounds, filter_bands, perturbation):
    kappa_field = jnp.zeros(kappa_index.shape, jnp.float32)
    for entry in range(kappa_table.shape[0]):
        kappa_field = kappa_field + jnp.where(kappa_index == entry, kappa_table[entry], 0.0)
    weights = face_weights(kappa_field)
    state_field = lax.fori_loop(0, ITERS, lambda step, cur: diffuse_step(cur, weights), control)
    flattened = state_field.reshape(state_field.shape[0], state_field.shape[1], -1)
    by_columns = lax.all_to_all(flattened, "geo", split_axis=2, concat_axis=1, tiled=True)
    width = by_columns.shape[2]
    tiles_count = filter_bands.shape[0]
    columns = lax.axis_index("geo") * width + jnp.arange(width, dtype=jnp.int32)
    tile_ids = jnp.sum((columns[None, :] >= tile_bounds[1:-1][:, None]).astype(jnp.int32), axis=0)
    one_hot = (tile_ids[None, :] == jnp.arange(tiles_count, dtype=jnp.int32)[:, None]).astype(
        jnp.float32
    )
    coefficients = jnp.einsum("tkl,tc->klc", filter_bands, one_hot, precision=lax.Precision.HIGHEST)
    filtered = vertical_filter(by_columns[0], coefficients).astype(jnp.bfloat16)
    products = perturbation[:, 0].astype(jnp.float32) * filtered.astype(jnp.float32)[None]
    return lax.psum_scatter(products, "mem", scatter_dimension=1, tiled=True)


def solution(mesh):
    in_specs = (P("mem", "geo", None, None), P(), P(), P(), P(), P(None, "mem", None, "geo"))
    out_specs = P(None, "mem", "geo")
    return jax.shard_map(body, mesh=mesh, in_specs=in_specs, out_specs=out_specs, check_vma=False)
```

profile of v0, /device:TPU:8, one launch (start us, length us, event | category | flops | bytes accessed | tf_op | source)
XLA Modules:
  0.0 340.9 jit_solution(5433511955447139947)
XLA Ops:
  6.5 0.9 copy.26
  7.5 1.9 fusion.35
  9.4 10.9 %select_add_fusion = f32[48,384]{1,0:T(8,128)S(1)} fusion(s32[48,384]{1,0:T(8,128)} %param.10, f32[]{:T(128)} %bitcast.16, f32[]{:T(128)} %bitcast.15, f32[]{:T(128)} %bitcast.14, f32[]{:T(128)} %bitcast.13, f32[]{:T(128)} %bitcast.12, f32[]{:T(128)} %bitcast.11, f32[]{:T(128)} %bitcast.10, f32[]{:T(128)} %bitcast.9, f32[]{:T(128)} %bitcast.8, f32[]{:T(128)} %bitcast.7, ...), kind=kLoop, calls=%fused_computation.44 | loop fusion | flops 866304 | bytes 147520 | tf_op jit(solution)/shard_map/add | solution.py:40
  20.5 11.0 %fusion.22 = (f32[48,384]{1,0:T(8,128)S(1)}, f32[48,384]{1,0:T(8,128)S(1)}, f32[48,384]{1,0:T(8,128)S(1)}, f32[48,384]{1,0:T(8,128)S(1)}) fusion(f32[48,383]{1,0:T(8,128)S(1)} %get-tuple-element.64, f32[48,1]{1,0:T(8,128)S(1)} %get-tuple-element.62, f32[48,1]{1,0:T(8,128)S(1)} %get-tuple-element.63, f32[48,383]{1,0:T(8,128)S(1)} %get-tuple-element.65, ...), kind=kLoop, calls=%fused_computation.41 | loop fusion | flops 1087488 | bytes 663616 | tf_op jit(solution)/shard_map/mul | solution.py:18
  31.5 4.1 %while.10 = (s32[]{:T(128)}, f32[1,2,48,384]{3,2,1,0:T(8,128)S(1)}, f32[48,384]{1,0:T(8,128)S(1)}, f32[48,384]{1,0:T(8,128)S(1)}, f32[48,384]{1,0:T(8,128)S(1)}, /*index=5*/f32[48,384]{1,0:T(8,128)S(1)}, s32[]{:T(128)}) while((s32[]{:T(128)}, f32[1,2,48,384]{3,2,1,0:T(8,128)S(1)}, f32[48,384]{1,0:T(8,128)S(1)}, f32[48,384]{1,0:T(8,128)S(1)}, ...), condition=%wide.region_1.2_spmd, body=%wide.region_0.1_spmd.sunk | while | flops 589826 | bytes 2359373 | solution.py:42
  31.7 0.2 fusion.46
  32.1 0.2 fusion.46
  33.4 0.2 fusion.46
  35.6 5.6 %copy.13 = f32[1,2,48,384]{1,3,2,0:T(8,128)} copy(f32[1,2,48,384]{3,2,1,0:T(8,128)S(1)} %get-tuple-element.37) | data formatting | bytes 294912 | tf_op jit(solution)/shard_map/while | solution.py:42
  41.2 0.5 broadcast.25
  41.7 83.6 %reduce = f32[18432,2]{1,0:T(8,128)} reduce(f32[18432,1,2]{2,1,0:T(1,128)} %bitcast.63, f32[]{:T(128)} %broadcast.25), dimensions={1}, to_apply=%bitcast.60.reduce_sub_computation | reduce | bytes 294916
  125.3 8.9 %reshape.29 = f32[16,1,2304]{2,1,0:T(1,128)} reshape(f32[18432,2]{1,0:T(8,128)} %reduce) | data formatting | bytes 294912
  134.1 9.1 %all-to-all-start = ((f32[16,1,2304]{2,1,0:T(1,128)}), f32[16,1,2304]{2,1,0:T(1,128)S(1)}, u32[]{:S(2)}, u32[]{:S(2)}) async-start(f32[16,1,2304]{2,1,0:T(1,128)} %reshape.29), calls=%async_computation | async-start | bytes 294912 | tf_op jit(solution)/shard_map/all_to_all | solution.py:44
  143.3 0.2 all-reduce.4.cloned.1.call-start
  143.7 0.5 convolution_bitcast_fusion
  144.2 6.8 %all-to-all-done = f32[16,1,2304]{2,1,0:T(1,128)S(1)} async-done(((f32[16,1,2304]{2,1,0:T(1,128)}), f32[16,1,2304]{2,1,0:T(1,128)S(1)}, u32[]{:S(2)}, u32[]{:S(2)}) %all-to-all-start) | async-done | bytes 147488 | tf_op jit(solution)/shard_map/all_to_all | solution.py:44
  151.0 1.0 reduce.1
  152.0 17.8 %reshape.30 = f32[18432,1,2]{2,1,0:T(1,128)} reshape(f32[16,2304]{1,0:T(8,128)S(1)} %reduce.1) | data formatting | bytes 294912
  169.9 5.6 %copy.14 = f32[1,2,16,1152]{3,1,2,0:T(2,128)S(1)} copy(f32[1,2,16,1152]{1,3,2,0:T(8,128)} %bitcast.64) | data formatting | bytes 294912 | tf_op jit(solution)/shard_map/all_to_all | solution.py:44
  175.7 0.9 convert_multiply_fusion
  176.6 1.3 dynamic-slice
  177.9 154.2 %all-reduce.4.cloned.1.call-done = f32[2,32,1152]{2,0,1:T(2,128)} async-done(((f32[2,32,1152]{2,0,1:T(2,128)}), f32[2,32,1152]{2,0,1:T(2,128)}) %all-reduce.4.cloned.1.call-update) | async-done | bytes 294928
  332.1 1.3 constant_dynamic-slice_fusion
  333.4 0.6 copy.15
  (63 shorter events, 3.7 us)
Async XLA Ops:
  6.5 137.2 %copy-start = (f32[16,5,32]{2,0,1:T(8,128)S(1)}, f32[16,5,32]{2,0,1:T(8,128)}, u32[]{:S(2)}) copy-start(f32[16,5,32]{2,0,1:T(8,128)} %param.12) | copy-start | bytes 30724
  125.2 18.3 %copy-start.2 = (s32[17]{0:T(128)S(1)}, s32[17]{0:T(128)}, u32[]{:S(2)}) copy-start(s32[17]{0:T(128)} %param.11) | copy-start | bytes 208
  134.1 16.9 %all-to-all-start = ((f32[16,1,2304]{2,1,0:T(1,128)}), f32[16,1,2304]{2,1,0:T(1,128)S(1)}, u32[]{:S(2)}, u32[]{:S(2)}) async-start(f32[16,1,2304]{2,1,0:T(1,128)} %reshape.29), calls=%async_computation | async-start | bytes 294912 | tf_op jit(solution)/shard_map/all_to_all | solution.py:44
  143.3 188.8 %all-reduce.4.cloned.1.call-start = ((), (), s32[]{:S(2)}) async-start(), calls=%async_computation.1 | async-start | bytes 589824
  152.0 23.7 %copy-start.1 = (bf16[2,1,32,1152]{3,2,1,0:T(8,128)(2,1)S(1)}, bf16[2,1,32,1152]{3,2,1,0:T(8,128)(2,1)}, u32[]{:S(2)}) copy-start(bf16[2,1,32,1152]{3,2,1,0:T(8,128)(2,1)} %param.13) | copy-start | bytes 442372
Sparse Core Ops, SparseCore 0:
  176.7 155.3 all-reduce.3
where the time goes:
time: 342 us; the launch traced here: 341 us
  waiting for transfers between devices  161 us (47%)
  other arithmetic  109 us (32%)
  local copies, waits for them, and re-layouts  47 us (14%)
  between operations  13.5 us (4%)
  starting transfers between devices  9.35 us (3%)
    unnamed x2, waiting for transfers between devices  154 us
    unnamed x1, other arithmetic  83.6 us
    unnamed x12, local copies, waits for them, and re-layouts  30.8 us
    mul x1, other arithmetic, face_weights(): 0.5 * (kappa_field + other)  11 us
    add x1, other arithmetic, body(): kappa_field + jnp.where(kappa_index == entry, kappa_table[entry], 0.0)  10.9 us
    all_to_all x1, starting transfers between devices, body(): lax.all_to_all(flattened, 'geo', split_axis=2, concat_axis=1, tiled=True)  9.13 us
  transfers between devices with their start and end apart: 2, of which 2 were waited for; matrix products, arithmetic and copies ran while one was open for 1% of the time, Pallas kernels for 0%

commit v1 on v0

--- a/solution.py
+++ b/solution.py
@@ -41,7 +41,10 @@
     weights = face_weights(kappa_field)
     state_field = lax.fori_loop(0, ITERS, lambda step, cur: diffuse_step(cur, weights), control)
     flattened = state_field.reshape(state_field.shape[0], state_field.shape[1], -1)
-    by_columns = lax.all_to_all(flattened, "geo", split_axis=2, concat_axis=1, tiled=True)
+    count = lax.axis_size("geo")
+    blocks = jnp.stack(jnp.split(flattened, count, axis=2), axis=0)
+    blocks = lax.all_to_all(blocks, "geo", split_axis=0, concat_axis=0)
+    by_columns = jnp.concatenate(blocks, axis=1)
     width = by_columns.shape[2]
     tiles_count = filter_bands.shape[0]
     columns = lax.axis_index("geo") * width + jnp.arange(width, dtype=jnp.int32)

time: 342 us -> 226 us (0.66)
  other arithmetic: 109 us -> 23.2 us
  local copies, waits for them, and re-layouts: 47 us -> 18.2 us
    unnamed x1 -> x0, other arithmetic: 83.6 us -> none
    unnamed x12 -> x29, local copies, waits for them, and re-layouts: 30.8 us -> 13.8 us
    while x1 -> x0, local copies, waits for them, and re-layouts: 5.61 us -> none  [body(): lax.fori_loop(0, ITERS, lambda step, cur: diffuse_step(cur, weights), con...]
    all_to_all x1 -> x0, local copies, waits for them, and re-layouts: 5.6 us -> none  [body(): lax.all_to_all(flattened, 'geo', split_axis=2, concat_axis=1, tiled=True)]
where the time goes in v1:
time: 226 us
  waiting for transfers between devices  161 us (71%)
  other arithmetic  23.2 us (10%)
  local copies, waits for them, and re-layouts  18.2 us (8%)
  between operations  13.5 us (6%)
  starting transfers between devices  9.17 us (4%)
    unnamed x2, waiting for transfers between devices  154 us
    unnamed x29, local copies, waits for them, and re-layouts  13.8 us
    mul x1, other arithmetic, face_weights(): 0.5 * (kappa_field + other)  10.3 us
    add x1, other arithmetic, body(): kappa_field + jnp.where(kappa_index == entry, kappa_table[entry], 0.0)  10.3 us
    all_to_all x1, starting transfers between devices, body(): blocks = lax.all_to_all(blocks, 'geo', split_axis=0, concat_axis=0)  9.13 us
    all_to_all x1, waiting for transfers between devices, body(): blocks = lax.all_to_all(blocks, 'geo', split_axis=0, concat_axis=0)  6.35 us
  transfers between devices with their start and end apart: 2, of which 2 were waited for; matrix products, arithmetic and copies ran while one was open for 1% of the time, Pallas kernels for 0%

profile of v1, /device:TPU:8, one launch (start us, length us, event | category | flops | bytes accessed | tf_op | source)
XLA Modules:
  0.0 225.7 jit_solution(3990329394365274593)
XLA Ops:
  6.5 0.7 copy-done.4
  7.2 0.7 fusion.35
  8.1 10.3 %select_add_fusion = f32[48,384]{1,0:T(8,128)S(1)} fusion(s32[48,384]{1,0:T(8,128)S(1)} %copy-done.2, f32[]{:T(128)} %bitcast.16, f32[]{:T(128)} %bitcast.15, f32[]{:T(128)} %bitcast.14, f32[]{:T(128)} %bitcast.13, f32[]{:T(128)} %bitcast.12, f32[]{:T(128)} %bitcast.11, f32[]{:T(128)} %bitcast.10, f32[]{:T(128)} %bitcast.9, f32[]{:T(128)} %bitcast.8, ...), kind=kLoop, calls=%fused_computation.44 | loop fusion | flops 866304 | bytes 147520 | tf_op jit(solution)/shard_map/add | solution.py:40
  18.6 10.3 %fusion.22 = (f32[48,384]{1,0:T(8,128)S(1)}, f32[48,384]{1,0:T(8,128)S(1)}, f32[48,384]{1,0:T(8,128)S(1)}, f32[48,384]{1,0:T(8,128)S(1)}) fusion(f32[48,383]{1,0:T(8,128)S(1)} %get-tuple-element.64, f32[48,1]{1,0:T(8,128)S(1)} %get-tuple-element.62, f32[48,1]{1,0:T(8,128)S(1)} %get-tuple-element.63, f32[48,383]{1,0:T(8,128)S(1)} %get-tuple-element.65, ...), kind=kLoop, calls=%fused_computation.41 | loop fusion | flops 1087488 | bytes 663616 | tf_op jit(solution)/shard_map/mul | solution.py:18
  28.9 4.0 %while.10 = (s32[]{:T(128)}, f32[1,2,48,384]{3,2,1,0:T(8,128)S(1)}, f32[48,384]{1,0:T(8,128)S(1)}, f32[48,384]{1,0:T(8,128)S(1)}, f32[48,384]{1,0:T(8,128)S(1)}, /*index=5*/f32[48,384]{1,0:T(8,128)S(1)}, s32[]{:T(128)}) while((s32[]{:T(128)}, f32[1,2,48,384]{3,2,1,0:T(8,128)S(1)}, f32[48,384]{1,0:T(8,128)S(1)}, f32[48,384]{1,0:T(8,128)S(1)}, ...), condition=%wide.region_1.2_spmd, body=%wide.region_0.1_spmd.sunk | while | flops 589826 | bytes 2359373 | solution.py:42
  33.0 0.6 constant_dynamic-update-slice_fusion.15
  33.6 0.6 constant_dynamic-update-slice_fusion.14
  35.4 0.6 constant_dynamic-update-slice_fusion.11
  36.0 0.6 constant_dynamic-update-slice_fusion.10
  36.6 0.6 constant_dynamic-update-slice_fusion.9
  37.2 0.6 constant_dynamic-update-slice_fusion.8
  38.4 0.6 constant_dynamic-update-slice_fusion.6
  39.0 0.6 constant_dynamic-update-slice_fusion.5
  39.6 0.6 constant_dynamic-update-slice_fusion.4
  40.8 0.6 constant_dynamic-update-slice_fusion.2
  42.6 9.1 %all-to-all-start = ((f32[16,1,2,1152]{3,2,1,0:T(2,128)}), f32[16,1,2,1152]{3,2,1,0:T(2,128)S(1)}, u32[]{:S(2)}, u32[]{:S(2)}) async-start(f32[16,1,2,1152]{3,2,1,0:T(2,128)} %constant_dynamic-update-slice_fusion), calls=%async_computation | async-start | bytes 294912 | tf_op jit(solution)/shard_map/all_to_all | solution.py:46
  51.8 0.6 copy-done.5
  53.1 6.3 %all-to-all-done = f32[16,1,2,1152]{3,2,1,0:T(2,128)S(1)} async-done(((f32[16,1,2,1152]{3,2,1,0:T(2,128)}), f32[16,1,2,1152]{3,2,1,0:T(2,128)S(1)}, u32[]{:S(2)}, u32[]{:S(2)}) %all-to-all-start) | async-done | bytes 147488 | tf_op jit(solution)/shard_map/all_to_all | solution.py:46
  59.7 0.8 copy-done.3
  60.5 0.9 convert_multiply_fusion
  61.3 1.3 dynamic-slice
  62.6 154.2 %all-reduce.4.cloned.1.call-done = f32[2,32,1152]{2,0,1:T(2,128)} async-done(((f32[2,32,1152]{2,0,1:T(2,128)}), f32[2,32,1152]{2,0,1:T(2,128)}) %all-reduce.4.cloned.1.call-update) | async-done | bytes 294928
  216.9 1.3 constant_dynamic-slice_fusion
  218.2 0.6 copy.26
  (78 shorter events, 8.5 us)
Async XLA Ops:
  6.5 46.0 %copy-start = (f32[16,5,32]{2,0,1:T(8,128)S(1)}, f32[16,5,32]{2,0,1:T(8,128)}, u32[]{:S(2)}) copy-start(f32[16,5,32]{2,0,1:T(8,128)} %param.12) | copy-start | bytes 30724
  6.5 0.7 copy-start.4
  7.2 0.9 copy-start.2
  18.5 10.4 %copy-start.1 = (f32[1,2,48,384]{3,2,1,0:T(8,128)S(1)}, f32[1,2,48,384]{3,2,1,0:T(8,128)}, u32[]{:S(2)}) copy-start(f32[1,2,48,384]{3,2,1,0:T(8,128)} %param.8) | copy-start | bytes 442372
  42.6 16.9 %all-to-all-start = ((f32[16,1,2,1152]{3,2,1,0:T(2,128)}), f32[16,1,2,1152]{3,2,1,0:T(2,128)S(1)}, u32[]{:S(2)}, u32[]{:S(2)}) async-start(f32[16,1,2,1152]{3,2,1,0:T(2,128)} %constant_dynamic-update-slice_fusion), calls=%async_computation | async-start | bytes 294912 | tf_op jit(solution)/shard_map/all_to_all | solution.py:46
  51.7 165.1 %all-reduce.4.cloned.1.call-start = ((), (), s32[]{:S(2)}) async-start(), calls=%async_computation.1 | async-start | bytes 589824
  51.8 0.7 copy-start.5
  59.5 0.9 copy-start.3
Sparse Core Ops, SparseCore 0:
  61.5 155.3 all-reduce.3
